TPU v7x, 32 devices: a whole 2x2x4 slice. The times are simulated.
32 devices in a mesh: grp: 4 (over x, core), dev: 8 (over z, y).
Axes of the slice: x: 2, y: 2, z: 4, core: 2. Of those that a mesh axis runs over, the one named last changes fastest.
Arguments:
- points: float32 [32768, 128], P(('grp', 'dev')), may hold values from -0.6 to 0.6
- weights: float32 [32768, 128], P(('grp', 'dev')), may hold values from -0.12 to 0.12
- skel_index: int32 [32, 128], P(('grp', 'dev')), may hold values from 0 to 1023
- projection: float32 [32, 128, 1024], P(('grp', 'dev')), may hold values from -0.1875 to 0.1875
- top_index: int32 [4, 256], P('grp'), may hold values from 0 to 1023
- subtree_projection: float32 [4, 256, 1024], P('grp', None, 'dev'), may hold values from -0.1875 to 0.1875
- near_leaf_mask: int32 [32, 3], P(('grp', 'dev')), may hold values from 0 to 1, as said below
Outputs:
- potential: float32 [32768, 128], P(('grp', 'dev'))
Inputs may be any that keep to these rules, and one draw needn't show every extreme that they name: `near_leaf_mask`: entry [l, 1] (the leaf itself) is 1; entries that name a leaf outside the subtree are 0.
All inputs are finite; a program needn't handle non-finite values.
Results may differ from a plain program's by a relative error of at most 0.0003.
Values sent between devices are 32-bit elements; how exact they have to be, the bound alone decides.
A program may use at most 64 MiB of HBM per device.

v0:
```python
import functools
import math

import jax
import jax.numpy as jnp
from jax import lax
from jax.experimental import pallas as pl
from jax.experimental.pallas import tpu as pltpu
from jax.sharding import PartitionSpec as P

F32 = jnp.float32
BF16 = jnp.bfloat16
ROOT = math.sqrt(math.log2(math.e))
TILE = 256
BLOCK = 512
CHUNKS = 4


def split2(x):
    hi = x.astype(BF16)
    return hi, (x - hi.astype(F32)).astype(BF16)


def split3(x):
    hi = x.astype(BF16)
    rest = x - hi.astype(F32)
    mid = rest.astype(BF16)
    return hi, mid, (rest - mid.astype(F32)).astype(BF16)


def dot(a, b, dims=((1,), (0,))):
    return lax.dot_general(a, b, (dims, ((), ())), preferred_element_type=F32)


def dot3(a, b):
    n = b.shape[1]
    ah, al = split2(a)
    bh, bl = split2(b)
    both = dot(ah, jnp.concatenate([bh, bl], axis=1))
    return both[:, :n] + both[:, n:] + dot(al, bh)


def norm_columns(x, first):
    rows, feats = x.shape
    norm = -0.5 * jnp.sum(x * x, axis=1, keepdims=True)
    parts = [v.astype(F32) for v in split3(norm)]
    lane = lax.broadcasted_iota(jnp.int32, (rows, feats), 1)
    out = jnp.where((lane >= 3 - first) & (lane < 6 - first), 1.0, 0.0).astype(F32)
    for i, part in enumerate(parts):
        out = jnp.where(lane == first + i, part, out)
    return out.astype(BF16)


def kernel(
    n_grp, n_dev,
    pts, wts, skel_idx, proj, top_idx, sub, mask, out,
    left, right, right_w, acc, near, skel, slab, top_p, top_w,
    near_send, near_recv, skel_send, skel_recv, slab_send, slab_recv,
    row_send, row_recv, tp_send, tp_recv, tw_send, tw_recv,
):
    leaf, feats = pts.shape
    rhs = wts.shape[1]
    n_skel = skel_idx.shape[1]
    n_top = top_idx.shape[1]
    top_rows = n_top // n_dev
    g = lax.axis_index("grp")
    p = lax.axis_index("dev")
    half = n_dev // 2
    h = p // 2
    odd = p % 2
    partner = p + 1 - 2 * odd
    step_rows = leaf // CHUNKS

    def remote(src, dst, send, recv, dev=None, grp=None):
        return pltpu.make_async_remote_copy(
            src_ref=src, dst_ref=dst, send_sem=send, recv_sem=recv,
            device_id=(g if grp is None else grp, p if dev is None else dev),
            device_id_type=pl.DeviceIdType.MESH,
        )

    barrier = pltpu.get_barrier_semaphore()
    dev_peers = [lax.rem(p + k, n_dev) for k in range(1, n_dev)]
    grp_peers = [lax.rem(g + k, n_grp) for k in range(1, n_grp)]
    for q in dev_peers:
        pl.semaphore_signal(barrier, inc=1, device_id=(g, q), device_id_type=pl.DeviceIdType.MESH)
    for q in grp_peers:
        pl.semaphore_signal(barrier, inc=1, device_id=(q, p), device_id_type=pl.DeviceIdType.MESH)
    pl.semaphore_wait(barrier, len(dev_peers) + len(grp_peers))

    ahead = p + 2 - 4 * odd
    behind = p - 2 + 4 * odd
    can_send = (ahead >= 0) & (ahead < n_dev)
    can_recv = (behind >= 0) & (behind < n_dev)

    def near_first(c, part):
        rows = pl.ds(c * step_rows, step_rows)
        src = pts if part == 0 else wts
        return remote(
            src.at[rows], near.at[0, part, rows],
            near_send.at[0, part, c], near_recv.at[0, part, c], dev=partner,
        )

    def near_second(c, part):
        rows = pl.ds(c * step_rows, step_rows)
        return remote(
            near.at[0, part, rows], near.at[1, part, rows],
            near_send.at[1, part, c], near_recv.at[1, part, c], dev=ahead,
        )

    def start_first(c):
        near_first(c, 0).start()
        near_first(c, 1).start()

    def pass_on(c):
        for part in range(2):
            near_first(c, part).wait_recv()

            @pl.when(can_send)
            def _():
                near_second(c, part).start()

    def wait_second(c):
        @pl.when(can_recv)
        def _():
            for part in range(2):
                near_second(c, part).wait_recv()

    def skel_copy(owner, way, dev):
        return remote(
            skel.at[owner], skel.at[owner], skel_send.at[way, owner], skel_recv.at[owner], dev=dev
        )

    def skel_up(owner):
        @pl.when(h + 1 < half)
        def _():
            skel_copy(owner, 0, p + 2).start()

    def skel_down(owner):
        @pl.when(h > 0)
        def _():
            skel_copy(owner, 1, p - 2).start()

    def skel_step(s):
        @pl.when(h - s >= 0)
        def _():
            for side in range(2):
                owner = 2 * (h - s) + side
                skel_copy(owner, 0, partner).wait_recv()
                skel_up(owner)

        @pl.when(h + s < half)
        def _():
            for side in range(2):
                owner = 2 * (h + s) + side
                skel_copy(owner, 1, partner).wait_recv()
                skel_down(owner)

    def slab_copy(q, owner):
        return remote(
            sub.at[0, pl.ds(pl.multiple_of(q * top_rows, top_rows), top_rows)],
            slab.at[owner], slab_send.at[q], slab_recv.at[owner], dev=q,
        )

    for q in dev_peers:
        slab_copy(q, p).start()
    start_first(0)

    row = lax.broadcasted_iota(jnp.int32, (leaf, n_skel), 0)
    pick = jnp.where(row == skel_idx[...], 1.0, 0.0).astype(BF16)
    picked = dot(pick, jnp.concatenate(split3(pts[...]), axis=1), ((0,), (0,)))
    skel[p, 0] = picked[:, :feats] + picked[:, feats:2 * feats] + picked[:, 2 * feats:]
    skel[p, 1] = dot3(proj[0], wts[...])
    skel_copy(p, 2, partner).start()
    skel_up(p)
    skel_down(p)
    start_first(1)

    a = pts[...] * ROOT
    ah, al = split2(a)
    left[:, :feats] = ah
    left[:, feats:2 * feats] = al
    left[:, 2 * feats:3 * feats] = ah
    left[:, 3 * feats:] = norm_columns(a, 0)
    acc[...] = jnp.zeros_like(acc)

    def apply(first, source, weight):
        rows = pl.ds(first, source.shape[0])
        b = source * ROOT
        bh, bl = split2(b)
        right[rows, :feats] = bh
        right[rows, feats:2 * feats] = bh
        right[rows, 2 * feats:3 * feats] = bl
        right[rows, 3 * feats:] = norm_columns(b, 3)
        wh, wl = split2(weight)
        right_w[rows, :rhs] = wh
        right_w[rows, rhs:] = wl

    def run(width):
        def tile(i, carry):
            rows = pl.ds(pl.multiple_of(i * TILE, TILE), TILE)
            k = jnp.exp2(dot(left[rows], right[:width], ((1,), (1,))))
            kh, kl = split2(k)
            w = right_w[:width]
            acc[rows] += dot(kh, w) + dot(kl, w)
            return carry

        lax.fori_loop(0, leaf // TILE, tile, 0)

    def near_scale(k):
        return mask[0, k].astype(F32)

    blocks = []

    def self_block(i):
        rows = pl.ds(i * BLOCK, BLOCK)
        apply(0, pts[rows], wts[rows] * near_scale(1))
        run(BLOCK)

    per = BLOCK // step_rows

    def partner_block(i):
        rows = pl.ds(i * BLOCK, BLOCK)
        scale = jnp.where(odd == 1, near_scale(0), near_scale(2))
        apply(0, near[0, 0, rows], near[0, 1, rows] * scale)
        run(BLOCK)

    def other_block(i):
        for c in range(i * per, (i + 1) * per):
            wait_second(c)

        @pl.when(can_recv)
        def _():
            rows = pl.ds(i * BLOCK, BLOCK)
            scale = jnp.where(odd == 1, near_scale(2), near_scale(0))
            apply(0, near[1, 0, rows], near[1, 1, rows] * scale)
            run(BLOCK)

    leaves = BLOCK // n_skel

    def far_block(i):
        for j in range(leaves):
            owner = i * leaves + j
            keep = jnp.float32(1.0)
            for k in range(3):
                keep = keep - jnp.where(owner == p - 1 + k, near_scale(k), 0.0)
            apply(j * n_skel, skel[owner, 0], skel[owner, 1] * keep)
        run(BLOCK)

    self_block(0)
    skel_copy(partner, 2, partner).wait_recv()
    skel_up(partner)
    skel_down(partner)
    pass_on(0)
    start_first(2)
    self_block(1)
    for s in range(1, half):
        skel_step(s)
        if s == 1:
            pass_on(1)
            start_first(3)
            partner_block(0)

    def top_pick(j, total):
        ids = lax.broadcasted_iota(jnp.int32, (n_skel, n_top), 0) + j * n_skel
        one = jnp.where(ids == top_idx[...], 1.0, 0.0).astype(BF16)
        got = dot(one, jnp.concatenate(split3(skel[j, 0]), axis=1), ((0,), (0,)))
        return total + (got[:, :feats] + got[:, feats:2 * feats] + got[:, 2 * feats:])

    top_p[g] = lax.fori_loop(0, n_dev, top_pick, jnp.zeros((n_top, feats), F32))
    for q in grp_peers:
        remote(top_p.at[g], top_p.at[g], tp_send.at[q], tp_recv.at[g], grp=q).start()
    for q in dev_peers:
        slab_copy(p, q).wait_recv()
    slab[p] = sub[0, pl.ds(pl.multiple_of(p * top_rows, top_rows), top_rows)]

    def top_weight(j, total):
        return total + dot3(slab[j], skel[j, 1])

    top_w[g, p] = lax.fori_loop(0, n_dev, top_weight, jnp.zeros((top_rows, rhs), F32))
    for q in dev_peers:
        remote(top_w.at[g, p], top_w.at[g, p], row_send.at[q], row_recv.at[p], dev=q).start()

    far_block(0)
    for q in dev_peers:
        remote(top_w.at[g, q], top_w.at[g, q], row_send.at[q], row_recv.at[q], dev=q).wait_recv()
    for q in grp_peers:
        remote(top_w.at[g], top_w.at[g], tw_send.at[q], tw_recv.at[g], grp=q).start()
    pass_on(2)
    far_rest = n_dev // leaves
    if far_rest > 1:
        @pl.loop(1, far_rest)
        def _(i):
            far_block(i)
    pass_on(3)
    partner_block(1)
    other_block(0)
    for q in grp_peers:
        remote(top_p.at[q], top_p.at[q], tp_send.at[q], tp_recv.at[q], grp=q).wait_recv()
        remote(top_w.at[q], top_w.at[q], tw_send.at[q], tw_recv.at[q], grp=q).wait_recv()
        apply(0, top_p[q], top_w[q].reshape(n_top, rhs))
        run(n_top)
    other_block(1)
    out[...] = acc[:, :rhs] + acc[:, rhs:]

    for c in range(CHUNKS):
        for part in range(2):
            near_first(c, part).wait_send()

            @pl.when(can_send)
            def _():
                near_second(c, part).wait_send()
    skel_copy(p, 2, partner).wait_send()

    @pl.when(h + 1 < half)
    def _():
        @pl.loop(0, 2 * h + 2)
        def _(owner):
            skel_copy(owner, 0, p + 2).wait_send()

    @pl.when(h > 0)
    def _():
        @pl.loop(2 * h, n_dev)
        def _(owner):
            skel_copy(owner, 1, p - 2).wait_send()

    for q in dev_peers:
        slab_copy(q, p).wait_send()
        remote(top_w.at[g, p], top_w.at[g, p], row_send.at[q], row_recv.at[p], dev=q).wait_send()
    for q in grp_peers:
        remote(top_p.at[g], top_p.at[g], tp_send.at[q], tp_recv.at[g], grp=q).wait_send()
        remote(top_w.at[g], top_w.at[g], tw_send.at[q], tw_recv.at[g], grp=q).wait_send()


def solution(mesh):
    n_grp, n_dev = mesh.shape["grp"], mesh.shape["dev"]

    def local(points, weights, skel_index, projection, top_index, subtree_projection, near_leaf_mask):
        leaf, feats = points.shape
        rhs = weights.shape[1]
        n_skel = skel_index.shape[1]
        n_top = top_index.shape[1]
        vmem = pl.BlockSpec(memory_space=pltpu.VMEM)
        dma = pltpu.SemaphoreType.DMA
        return pl.pallas_call(
            functools.partial(kernel, n_grp, n_dev),
            out_shape=jax.ShapeDtypeStruct((leaf, rhs), F32),
            in_specs=[vmem] * 6 + [pl.BlockSpec(memory_space=pltpu.SMEM)],
            out_specs=vmem,
            scratch_shapes=[
                pltpu.VMEM((leaf, 4 * feats), BF16),
                pltpu.VMEM((BLOCK, 4 * feats), BF16),
                pltpu.VMEM((BLOCK, 2 * rhs), BF16),
                pltpu.VMEM((leaf, 2 * rhs), F32),
                pltpu.VMEM((2, 2, leaf, feats), F32),
                pltpu.VMEM((n_dev, 2, n_skel, feats), F32),
                pltpu.VMEM((n_dev, n_top // n_dev, n_skel), F32),
                pltpu.VMEM((n_grp, n_top, feats), F32),
                pltpu.VMEM((n_grp, n_dev, n_top // n_dev, rhs), F32),
                dma((2, 2, CHUNKS)), dma((2, 2, CHUNKS)),
                dma((3, n_dev)), dma((n_dev,)),
                dma((n_dev,)), dma((n_dev,)),
                dma((n_dev,)), dma((n_dev,)),
                dma((n_grp,)), dma((n_grp,)),
                dma((n_grp,)), dma((n_grp,)),
            ],
            compiler_params=pltpu.CompilerParams(
                collective_id=0, has_side_effects=True, vmem_limit_bytes=48 * 1024 * 1024
            ),
        )(points, weights, skel_index, projection, top_index, subtree_projection, near_leaf_mask)

    return jax.shard_map(
        local,
        mesh=mesh,
        in_specs=(
            P(("grp", "dev"), None),
            P(("grp", "dev"), None),
            P(("grp", "dev"), None),
            P(("grp", "dev"), None, None),
            P("grp", None),
            P("grp", None, "dev"),
            P(("grp", "dev"), None),
        ),
        out_specs=P(("grp", "dev"), None),
        check_vma=False,
    )
```

profile of v0, /device:TPU:4, one launch (start us, length us, event | category | flops | bytes accessed | tf_op | source)
XLA Modules:
  0.0 78.3 jit_solution(17675599687133242579)
XLA Ops:
  0.0 0.0 copy-start
  0.0 1.0 %copy-done = f32[1024,128]{1,0:T(8,128)S(1)} copy-done((f32[1024,128]{1,0:T(8,128)S(1)}, f32[1024,128]{1,0:T(8,128)}, u32[]{:S(2)}) %copy-start) | copy-done | bytes 524312
  1.0 0.0 copy-start.1
  1.0 1.0 %copy-done.1 = f32[1024,128]{1,0:T(8,128)S(1)} copy-done((f32[1024,128]{1,0:T(8,128)S(1)}, f32[1024,128]{1,0:T(8,128)}, u32[]{:S(2)}) %copy-start.1) | copy-done | bytes 524312
  2.1 0.0 copy-start.2
  2.1 1.0 %copy-done.2 = f32[1,128,1024]{2,1,0:T(8,128)S(1)} copy-done((f32[1,128,1024]{2,1,0:T(8,128)S(1)}, f32[1,128,1024]{2,1,0:T(8,128)}, u32[]{:S(2)}) %copy-start.2) | copy-done | bytes 524312
  3.1 0.0 copy-start.3
  3.1 0.9 %copy-done.3 = f32[1,256,128]{2,1,0:T(8,128)S(1)} copy-done((f32[1,256,128]{2,1,0:T(8,128)S(1)}, f32[1,256,128]{2,1,0:T(8,128)}, u32[]{:S(2)}) %copy-start.3) | copy-done | bytes 131096
  4.0 0.0 copy-start.4
  4.0 0.7 copy-done.4
  4.7 0.0 copy-start.5
  4.7 0.7 copy-done.5
  5.4 0.0 copy-start.6
  5.4 0.7 copy-done.6
  6.0 71.5 %shard_map.73 = f32[1024,128]{1,0:T(8,128)S(1)} custom-call(f32[1024,128]{1,0:T(8,128)S(1)} %copy-done, f32[1024,128]{1,0:T(8,128)S(1)} %copy-done.1, s32[1,128]{1,0:T(1,128)S(1)} %copy-done.5, f32[1,128,1024]{2,1,0:T(8,128)S(1)} %copy-done.2, s32[1,256]{1,0:T(1,128)S(1)} %copy-done.4, f32[1,256,128]{2,1,0:T(8,128)S(1)} %copy-done.3, s32[1,3]{1,0:T(1,128)S(1)} %copy-done.6), custom_call_target="tpu_custom_call" | custom-call | tf_op jit(solution)/shard_map/pallas_call | solution.py:344
  77.5 0.8 %copy.9 = f32[1024,128]{1,0:T(8,128)} copy(f32[1024,128]{1,0:T(8,128)S(1)} %shard_map.73) | data formatting | bytes 1048576
Async XLA Ops:
  0.0 1.0 %copy-start = (f32[1024,128]{1,0:T(8,128)S(1)}, f32[1024,128]{1,0:T(8,128)}, u32[]{:S(2)}) copy-start(f32[1024,128]{1,0:T(8,128)} %pts.1) | copy-start | bytes 1572868
  1.0 1.0 %copy-start.1 = (f32[1024,128]{1,0:T(8,128)S(1)}, f32[1024,128]{1,0:T(8,128)}, u32[]{:S(2)}) copy-start(f32[1024,128]{1,0:T(8,128)} %wts.1) | copy-start | bytes 1572868
  2.1 1.0 %copy-start.2 = (f32[1,128,1024]{2,1,0:T(8,128)S(1)}, f32[1,128,1024]{2,1,0:T(8,128)}, u32[]{:S(2)}) copy-start(f32[1,128,1024]{2,1,0:T(8,128)} %proj.1) | copy-start | bytes 1572868
  3.1 0.9 %copy-start.3 = (f32[1,256,128]{2,1,0:T(8,128)S(1)}, f32[1,256,128]{2,1,0:T(8,128)}, u32[]{:S(2)}) copy-start(f32[1,256,128]{2,1,0:T(8,128)} %sub.1) | copy-start | bytes 393220
  4.0 0.7 copy-start.4
  4.7 0.7 copy-start.5
  5.4 0.7 copy-start.6
where the time goes:
time: 78.6 us; the launch traced here: 78.3 us
  Pallas kernels  71.5 us (91%)
  local copies, waits for them, and re-layouts  6.81 us (9%)
    pallas_call x1, Pallas kernels, local(): pl.pallas_call(functools.partial(kernel, n_grp, n_dev), out_shape=jax.Sha...  71.5 us
    unnamed x15, local copies, waits for them, and re-layouts  6.81 us

commit v1 on v0

--- a/solution.py
+++ b/solution.py
@@ -53,9 +53,10 @@
 
 def kernel(
     n_grp, n_dev,
-    pts, wts, skel_idx, proj, top_idx, sub, mask, out,
-    left, right, right_w, acc, near, skel, slab, top_p, top_w,
-    near_send, near_recv, skel_send, skel_recv, slab_send, slab_recv,
+    pts_in, wts_in, skel_idx_in, proj_in, top_idx_in, sub_in, mask_in, out,
+    pts, wts, skel_idx, proj, top_idx, sub, mask,
+    left, right, right_w, acc, near, skel, part_w, slab, top_p, top_w,
+    load, near_send, near_recv, skel_send, skel_recv, slab_send, slab_recv,
     row_send, row_recv, tp_send, tp_recv, tw_send, tw_recv,
 ):
     leaf, feats = pts.shape
@@ -78,6 +79,15 @@
             device_id_type=pl.DeviceIdType.MESH,
         )
 
+    loads = [
+        pltpu.make_async_copy(src, dst, load.at[i])
+        for i, (src, dst) in enumerate(
+            [(skel_idx_in, skel_idx), (pts_in, pts), (proj_in, proj), (wts_in, wts),
+             (sub_in, sub), (top_idx_in, top_idx), (mask_in, mask)]
+        )
+    ]
+    for copy in loads:
+        copy.start()
     barrier = pltpu.get_barrier_semaphore()
     dev_peers = [lax.rem(p + k, n_dev) for k in range(1, n_dev)]
     grp_peers = [lax.rem(g + k, n_grp) for k in range(1, n_grp)]
@@ -94,7 +104,7 @@
 
     def near_first(c, part):
         rows = pl.ds(c * step_rows, step_rows)
-        src = pts if part == 0 else wts
+        src = pts_in if part == 0 else wts_in
         return remote(
             src.at[rows], near.at[0, part, rows],
             near_send.at[0, part, c], near_recv.at[0, part, c], dev=partner,
@@ -156,14 +166,58 @@
                 skel_down(owner)
 
     def slab_copy(q, owner):
+        return remote(part_w.at[q], slab.at[owner], slab_send.at[q], slab_recv.at[owner], dev=q)
+
+    def row_copy(q, owner):
         return remote(
-            sub.at[0, pl.ds(pl.multiple_of(q * top_rows, top_rows), top_rows)],
-            slab.at[owner], slab_send.at[q], slab_recv.at[owner], dev=q,
-        )
-
-    for q in dev_peers:
-        slab_copy(q, p).start()
+            top_w.at[g, owner], top_w.at[g, owner], row_send.at[q], row_recv.at[owner], dev=q
+        )
+
+    relay = n_grp == 4
+    mate = g + 1 - 2 * (g % 2)
+    across = lax.rem(g + 2, 4)
+    far_mate = lax.rem(mate + 2, 4)
+
+    def grp_copy(top, sems, q, owner, slot):
+        return remote(top.at[owner], top.at[owner], sems[0].at[slot], sems[1].at[owner], grp=q)
+
+    tp_sems, tw_sems = (tp_send, tp_recv), (tw_send, tw_recv)
+
+    def grp_start(top, sems):
+        if relay:
+            grp_copy(top, sems, across, g, 1).start()
+            grp_copy(top, sems, mate, g, 0).start()
+        else:
+            for q in grp_peers:
+                grp_copy(top, sems, q, g, q).start()
+
+    def grp_relay(top, sems):
+        if relay:
+            grp_copy(top, sems, across, across, 1).wait_recv()
+            grp_copy(top, sems, mate, across, 2).start()
+
+    def grp_wait(top, sems, k):
+        if relay:
+            if k > 0:
+                owner = (mate, far_mate)[k - 1]
+                grp_copy(top, sems, mate, owner, 0).wait_recv()
+        else:
+            grp_copy(top, sems, grp_peers[k], grp_peers[k], grp_peers[k]).wait_recv()
+
+    grp_order = [across, mate, far_mate] if relay else grp_peers
+
+    def grp_sent(top, sems):
+        if relay:
+            grp_copy(top, sems, across, g, 1).wait_send()
+            grp_copy(top, sems, mate, g, 0).wait_send()
+            grp_copy(top, sems, mate, across, 2).wait_send()
+        else:
+            for q in grp_peers:
+                grp_copy(top, sems, q, g, q).wait_send()
+
     start_first(0)
+    for copy in loads:
+        copy.wait()
 
     row = lax.broadcasted_iota(jnp.int32, (leaf, n_skel), 0)
     pick = jnp.where(row == skel_idx[...], 1.0, 0.0).astype(BF16)
@@ -173,6 +227,9 @@
     skel_copy(p, 2, partner).start()
     skel_up(p)
     skel_down(p)
+    part_w[...] = dot3(sub[0], skel[p, 1]).reshape(n_dev, top_rows, rhs)
+    for q in dev_peers:
+        slab_copy(q, p).start()
     start_first(1)
 
     a = pts[...] * ROOT
@@ -204,7 +261,7 @@
             acc[rows] += dot(kh, w) + dot(kl, w)
             return carry
 
-        lax.fori_loop(0, leaf // TILE, tile, 0)
+        lax.fori_loop(0, leaf // TILE, tile, 0, unroll=True)
 
     def near_scale(k):
         return mask[0, k].astype(F32)
@@ -252,12 +309,23 @@
     skel_down(partner)
     pass_on(0)
     start_first(2)
+    total = part_w[p]
+    for q in dev_peers:
+        slab_copy(p, q).wait_recv()
+        total = total + slab[q]
+    top_w[g, p] = total
+    for q in dev_peers:
+        row_copy(q, p).start()
     self_block(1)
-    for s in range(1, half):
+    skel_step(1)
+    pass_on(1)
+    start_first(3)
+    for q in dev_peers:
+        row_copy(q, q).wait_recv()
+    grp_start(top_w, tw_sems)
+    for s in range(2, half):
         skel_step(s)
-        if s == 1:
-            pass_on(1)
-            start_first(3)
+        if s == 2:
             partner_block(0)
 
     def top_pick(j, total):
@@ -267,36 +335,21 @@
         return total + (got[:, :feats] + got[:, feats:2 * feats] + got[:, 2 * feats:])
 
     top_p[g] = lax.fori_loop(0, n_dev, top_pick, jnp.zeros((n_top, feats), F32))
-    for q in grp_peers:
-        remote(top_p.at[g], top_p.at[g], tp_send.at[q], tp_recv.at[g], grp=q).start()
-    for q in dev_peers:
-        slab_copy(p, q).wait_recv()
-    slab[p] = sub[0, pl.ds(pl.multiple_of(p * top_rows, top_rows), top_rows)]
-
-    def top_weight(j, total):
-        return total + dot3(slab[j], skel[j, 1])
-
-    top_w[g, p] = lax.fori_loop(0, n_dev, top_weight, jnp.zeros((top_rows, rhs), F32))
-    for q in dev_peers:
-        remote(top_w.at[g, p], top_w.at[g, p], row_send.at[q], row_recv.at[p], dev=q).start()
-
-    far_block(0)
-    for q in dev_peers:
-        remote(top_w.at[g, q], top_w.at[g, q], row_send.at[q], row_recv.at[q], dev=q).wait_recv()
-    for q in grp_peers:
-        remote(top_w.at[g], top_w.at[g], tw_send.at[q], tw_recv.at[g], grp=q).start()
+    grp_start(top_p, tp_sems)
+    grp_relay(top_w, tw_sems)
     pass_on(2)
-    far_rest = n_dev // leaves
-    if far_rest > 1:
-        @pl.loop(1, far_rest)
-        def _(i):
-            far_block(i)
+
+    @pl.loop(0, n_dev // leaves)
+    def _(i):
+        far_block(i)
+
+    grp_relay(top_p, tp_sems)
+    other_block(0)
     pass_on(3)
     partner_block(1)
-    other_block(0)
-    for q in grp_peers:
-        remote(top_p.at[q], top_p.at[q], tp_send.at[q], tp_recv.at[q], grp=q).wait_recv()
-        remote(top_w.at[q], top_w.at[q], tw_send.at[q], tw_recv.at[q], grp=q).wait_recv()
+    for k, q in enumerate(grp_order):
+        grp_wait(top_p, tp_sems, k)
+        grp_wait(top_w, tw_sems, k)
         apply(0, top_p[q], top_w[q].reshape(n_top, rhs))
         run(n_top)
     other_block(1)
@@ -325,10 +378,9 @@
 
     for q in dev_peers:
         slab_copy(q, p).wait_send()
-        remote(top_w.at[g, p], top_w.at[g, p], row_send.at[q], row_recv.at[p], dev=q).wait_send()
-    for q in grp_peers:
-        remote(top_p.at[g], top_p.at[g], tp_send.at[q], tp_recv.at[g], grp=q).wait_send()
-        remote(top_w.at[g], top_w.at[g], tw_send.at[q], tw_recv.at[g], grp=q).wait_send()
+        row_copy(q, p).wait_send()
+    grp_sent(top_p, tp_sems)
+    grp_sent(top_w, tw_sems)
 
 
 def solution(mesh):
@@ -340,22 +392,32 @@
         n_skel = skel_index.shape[1]
         n_top = top_index.shape[1]
         vmem = pl.BlockSpec(memory_space=pltpu.VMEM)
+        hbm = pl.BlockSpec(memory_space=pltpu.HBM)
         dma = pltpu.SemaphoreType.DMA
         return pl.pallas_call(
             functools.partial(kernel, n_grp, n_dev),
             out_shape=jax.ShapeDtypeStruct((leaf, rhs), F32),
-            in_specs=[vmem] * 6 + [pl.BlockSpec(memory_space=pltpu.SMEM)],
+            in_specs=[hbm] * 7,
             out_specs=vmem,
             scratch_shapes=[
+                pltpu.VMEM(points.shape, F32),
+                pltpu.VMEM(weights.shape, F32),
+                pltpu.VMEM(skel_index.shape, jnp.int32),
+                pltpu.VMEM(projection.shape, F32),
+                pltpu.VMEM(top_index.shape, jnp.int32),
+                pltpu.VMEM(subtree_projection.shape, F32),
+                pltpu.SMEM(near_leaf_mask.shape, jnp.int32),
                 pltpu.VMEM((leaf, 4 * feats), BF16),
                 pltpu.VMEM((BLOCK, 4 * feats), BF16),
                 pltpu.VMEM((BLOCK, 2 * rhs), BF16),
                 pltpu.VMEM((leaf, 2 * rhs), F32),
                 pltpu.VMEM((2, 2, leaf, feats), F32),
                 pltpu.VMEM((n_dev, 2, n_skel, feats), F32),
-                pltpu.VMEM((n_dev, n_top // n_dev, n_skel), F32),
+                pltpu.VMEM((n_dev, n_top // n_dev, rhs), F32),
+                pltpu.VMEM((n_dev, n_top // n_dev, rhs), F32),
                 pltpu.VMEM((n_grp, n_top, feats), F32),
                 pltpu.VMEM((n_grp, n_dev, n_top // n_dev, rhs), F32),
+                dma((7,)),
                 dma((2, 2, CHUNKS)), dma((2, 2, CHUNKS)),
                 dma((3, n_dev)), dma((n_dev,)),
                 dma((n_dev,)), dma((n_dev,)),

time: 78.6 us -> 67.8 us (0.86)
  Pallas kernels: 71.5 us -> 60.7 us
    pallas_call x1, Pallas kernels: 71.5 us -> 60.7 us  [local(): pl.pallas_call(functools.partial(kernel, n_grp, n_dev), out_shape=jax.Sha...]
where the time goes in v1:
time: 67.8 us; the launch traced here: 67.5 us
  Pallas kernels  60.7 us (90%)
  local copies, waits for them, and re-layouts  6.81 us (10%)
    pallas_call x1, Pallas kernels, local(): pl.pallas_call(functools.partial(kernel, n_grp, n_dev), out_shape=jax.Sha...  60.7 us
    unnamed x15, local copies, waits for them, and re-layouts  6.81 us

profile of v1, /device:TPU:4, one launch (start us, length us, event | category | flops | bytes accessed | tf_op | source)
XLA Modules:
  0.0 67.5 jit_solution(13026315243816570874)
XLA Ops:
  0.0 0.0 copy-start
  0.0 1.0 %copy-done = f32[1024,128]{1,0:T(8,128)S(1)} copy-done((f32[1024,128]{1,0:T(8,128)S(1)}, f32[1024,128]{1,0:T(8,128)}, u32[]{:S(2)}) %copy-start) | copy-done | bytes 524312
  1.0 0.0 copy-start.1
  1.0 1.0 %copy-done.1 = f32[1024,128]{1,0:T(8,128)S(1)} copy-done((f32[1024,128]{1,0:T(8,128)S(1)}, f32[1024,128]{1,0:T(8,128)}, u32[]{:S(2)}) %copy-start.1) | copy-done | bytes 524312
  2.1 0.0 copy-start.2
  2.1 1.0 %copy-done.2 = f32[1,128,1024]{2,1,0:T(8,128)S(1)} copy-done((f32[1,128,1024]{2,1,0:T(8,128)S(1)}, f32[1,128,1024]{2,1,0:T(8,128)}, u32[]{:S(2)}) %copy-start.2) | copy-done | bytes 524312
  3.1 0.0 copy-start.3
  3.1 0.9 %copy-done.3 = f32[1,256,128]{2,1,0:T(8,128)S(1)} copy-done((f32[1,256,128]{2,1,0:T(8,128)S(1)}, f32[1,256,128]{2,1,0:T(8,128)}, u32[]{:S(2)}) %copy-start.3) | copy-done | bytes 131096
  4.0 0.0 copy-start.4
  4.0 0.7 %copy-done.4 = s32[1,256]{1,0:T(1,128)S(1)} copy-done((s32[1,256]{1,0:T(1,128)S(1)}, s32[1,256]{1,0:T(1,128)}, u32[]{:S(2)}) %copy-start.4) | copy-done | bytes 1048
  4.7 0.0 copy-start.5
  4.7 0.7 copy-done.5
  5.4 0.0 copy-start.6
  5.4 0.7 copy-done.6
  6.0 60.7 %shard_map.73 = f32[1024,128]{1,0:T(8,128)S(1)} custom-call(f32[1024,128]{1,0:T(8,128)S(1)} %copy-done, f32[1024,128]{1,0:T(8,128)S(1)} %copy-done.1, s32[1,128]{1,0:T(1,128)S(1)} %copy-done.5, f32[1,128,1024]{2,1,0:T(8,128)S(1)} %copy-done.2, s32[1,256]{1,0:T(1,128)S(1)} %copy-done.4, f32[1,256,128]{2,1,0:T(8,128)S(1)} %copy-done.3, s32[1,3]{1,0:T(1,128)S(1)} %copy-done.6), custom_call_target="tpu_custom_call" | custom-call | tf_op jit(solution)/shard_map/pallas_call | solution.py:397
  66.7 0.8 %copy.9 = f32[1024,128]{1,0:T(8,128)} copy(f32[1024,128]{1,0:T(8,128)S(1)} %shard_map.73) | data formatting | bytes 1048576
Async XLA Ops:
  0.0 1.0 %copy-start = (f32[1024,128]{1,0:T(8,128)S(1)}, f32[1024,128]{1,0:T(8,128)}, u32[]{:S(2)}) copy-start(f32[1024,128]{1,0:T(8,128)} %pts_in.1) | copy-start | bytes 1572868
  1.0 1.0 %copy-start.1 = (f32[1024,128]{1,0:T(8,128)S(1)}, f32[1024,128]{1,0:T(8,128)}, u32[]{:S(2)}) copy-start(f32[1024,128]{1,0:T(8,128)} %wts_in.1) | copy-start | bytes 1572868
  2.1 1.0 %copy-start.2 = (f32[1,128,1024]{2,1,0:T(8,128)S(1)}, f32[1,128,1024]{2,1,0:T(8,128)}, u32[]{:S(2)}) copy-start(f32[1,128,1024]{2,1,0:T(8,128)} %proj_in.1) | copy-start | bytes 1572868
  3.1 0.9 %copy-start.3 = (f32[1,256,128]{2,1,0:T(8,128)S(1)}, f32[1,256,128]{2,1,0:T(8,128)}, u32[]{:S(2)}) copy-start(f32[1,256,128]{2,1,0:T(8,128)} %sub_in.1) | copy-start | bytes 393220
  4.0 0.7 %copy-start.4 = (s32[1,256]{1,0:T(1,128)S(1)}, s32[1,256]{1,0:T(1,128)}, u32[]{:S(2)}) copy-start(s32[1,256]{1,0:T(1,128)} %top_idx_in.1) | copy-start | bytes 3076
  4.7 0.7 copy-start.5
  5.4 0.7 copy-start.6
